TPU v7x, 32 devices: a whole 2x2x4 slice. The times are simulated.
32 devices in a mesh: scan: 2 (over y), wide: 8 (over z, x), narrow: 2 (over core).
Axes of the slice: x: 2, y: 2, z: 4, core: 2. Of those that a mesh axis runs over, the one named last changes fastest.
Arguments:
- projections: float32 [32, 512, 512], P(('scan', 'wide', 'narrow')), parts along dimension 0, may hold values from 0.2 to 1
- angle_index: int32 [32], P('scan'), parts along dimension 0, may hold values from 0 to 15, each once
Outputs:
- volume: float32 [1024, 64, 128], P(('scan', 'wide'), 'narrow'), parts along dimension 0
There are 2 independent parts, one for each index of `scan`. A program takes and returns all parts, laid end to end along the dimension named above; each array names one. Nothing has to cross between parts.
Inputs may be any that keep to these rules, and one draw needn't show every extreme that they name: `angle_index`: each angle number appears exactly once.
All inputs are finite; a program needn't handle non-finite values.
Results may differ from a plain program's by a relative error of at most 0.0003.
Values sent between devices are 32-bit elements; how exact they have to be, the bound alone decides.
A program may use at most 192 MiB of HBM per device.

v0:
```python
import math

import jax
import jax.numpy as jnp
from jax import lax
from jax.sharding import PartitionSpec as P

XV = 128
YV = 64
STEPS = 4


paganin_strength = 0.25
attenuation = 0.01
contrast = 0.8
time_step = 0.15
block_angles = 8
highest = lax.Precision.HIGHEST


def extended(cells, sides, width):
    for axis, dim in sides:
        count = lax.axis_size(axis)
        ends = count - 1
        head = lax.slice_in_dim(cells, 0, width, axis=dim)
        tail = lax.slice_in_dim(cells, cells.shape[dim] - width, cells.shape[dim], axis=dim)
        cells = jnp.concatenate(
            [
                lax.ppermute(tail, axis, [(i, (i + 1) % count) for i in range(ends)]),
                cells,
                lax.ppermute(head, axis, [((i + 1) % count, i) for i in range(ends)]),
            ],
            axis=dim,
        )
    return cells


def cosine_tables(n_points):
    grid_ints = jnp.arange(n_points, dtype=jnp.int32)
    phase_ints = grid_ints[:, None] * grid_ints[None, :] % n_points
    phase_angle = phase_ints.astype(jnp.float32) * (2.0 * math.pi / n_points)
    return (jnp.cos(phase_angle), jnp.sin(phase_angle))


def paganin_symbol(row_count, col_count):
    row_sin = jnp.sin(jnp.arange(row_count, dtype=jnp.float32) * (math.pi / row_count))
    col_sin = jnp.sin(jnp.arange(col_count, dtype=jnp.float32) * (math.pi / col_count))
    spectral = 4.0 * row_sin[:, None] ** 2 + 4.0 * col_sin[None, :] ** 2
    return 1.0 / (1.0 + paganin_strength * spectral)


def ramp_kernel(col_count):
    grid_ints = jnp.arange(col_count, dtype=jnp.int32)
    offset = grid_ints[:, None] - grid_ints[None, :]
    is_odd = offset % 2 != 0
    safe_dist = jnp.where(is_odd, offset.astype(jnp.float32), jnp.float32(1.0))
    odd_value = -1.0 / (math.pi * safe_dist) ** 2
    return jnp.where(offset == 0, jnp.float32(0.25), jnp.where(is_odd, odd_value, jnp.float32(0.0)))


def apply_ramp(stack, kernel):
    return jnp.einsum(
        "abc,cd->abd", stack, kernel, precision=highest, preferred_element_type=jnp.float32
    )


def phase_retrieve(projections):
    row_count, col_count = (projections.shape[1], projections.shape[2])
    row_cos, row_sin = cosine_tables(row_count)
    col_cos, col_sin = cosine_tables(col_count)
    col_pair = jnp.concatenate([col_cos, col_sin], axis=1)
    row_pair = jnp.concatenate([row_cos, row_sin], axis=0)
    col_section = jnp.einsum(
        "arc,cd->ard", projections, col_pair, precision=highest, preferred_element_type=jnp.float32
    )
    row_section = jnp.einsum(
        "mr,ard->amd", row_pair, col_section, precision=highest, preferred_element_type=jnp.float32
    )
    cos_left = row_section[:, :row_count, :col_count]
    cos_right = row_section[:, :row_count, col_count:]
    sin_left = row_section[:, row_count:, :col_count]
    sin_right = row_section[:, row_count:, col_count:]
    symbol = paganin_symbol(row_count, col_count)
    real_part = symbol * (cos_left - sin_right)
    imag_part = -symbol * (cos_right + sin_left)
    spectrum = jnp.concatenate([real_part, imag_part], axis=2)
    back_section = jnp.einsum(
        "mr,ard->amd", row_pair, spectrum, precision=highest, preferred_element_type=jnp.float32
    )
    upper_part = back_section[:, :row_count, :col_count] - back_section[:, row_count:, col_count:]
    lower_part = back_section[:, row_count:, :col_count] + back_section[:, :row_count, col_count:]
    back_pair = jnp.concatenate([col_cos, -col_sin], axis=0)
    joined = jnp.concatenate([upper_part, lower_part], axis=2)
    smooth = jnp.einsum(
        "ard,dc->arc", joined, back_pair, precision=highest, preferred_element_type=jnp.float32
    )
    smooth = smooth / (row_count * col_count)
    return -jnp.log(smooth) / attenuation


def back_project(sinograms, thetas, y_count, x_width):
    angle_count, slices, col_count = sinograms.shape
    x_coords = jnp.arange(x_width, dtype=jnp.float32) - 0.5 * x_width + 0.5
    y_coords = jnp.arange(y_count, dtype=jnp.int32).astype(jnp.float32) - 0.5 * YV + 0.5
    block_count = angle_count // block_angles
    sino_blocks = sinograms.reshape(block_count, block_angles, slices, col_count)
    theta_blocks = thetas.reshape(block_count, block_angles)

    def one_angle(row_data, index_row):
        return (jnp.take(row_data, index_row, axis=1), jnp.take(row_data, index_row + 1, axis=1))

    def add_block(block_index, accum_sum):
        sino_block = lax.dynamic_index_in_dim(sino_blocks, block_index, 0, keepdims=False)
        theta_block = lax.dynamic_index_in_dim(theta_blocks, block_index, 0, keepdims=False)
        position = (
            jnp.cos(theta_block)[:, None, None] * x_coords[None, None, :]
            + jnp.sin(theta_block)[:, None, None] * y_coords[None, :, None]
            + (0.5 * col_count - 0.5)
        )
        lower_pos = jnp.floor(position)
        fraction = (position - lower_pos).reshape(block_angles, 1, -1)
        lower_index = lower_pos.astype(jnp.int32).reshape(block_angles, -1)
        left_vals, right_vals = jax.vmap(one_angle)(sino_block, lower_index)
        values = (1.0 - fraction) * left_vals + fraction * right_vals
        return accum_sum + jnp.sum(values, axis=0).reshape(slices, y_count, x_width)

    start_sum = jnp.zeros((slices, y_count, x_width), jnp.float32)
    return lax.fori_loop(0, block_count, add_block, start_sum)


def conduct(diff):
    return diff / (1.0 + (diff / contrast) ** 2)


def diffuse_step(padded, z_first, y_first, row_count):
    z_cells, y_cells = (padded.shape[0], padded.shape[1])
    z_global = z_first + jnp.arange(z_cells, dtype=jnp.int32)
    y_global = y_first + jnp.arange(y_cells, dtype=jnp.int32)
    z_valid = ((z_global >= 0) & (z_global < row_count)).astype(jnp.float32)
    y_valid = ((y_global >= 0) & (y_global < YV)).astype(jnp.float32)
    centre = padded[1:-1, 1:-1]
    update = conduct(padded[2:, 1:-1] - centre) * z_valid[2:, None, None]
    update = update + conduct(padded[:-2, 1:-1] - centre) * z_valid[:-2, None, None]
    update = update + conduct(padded[1:-1, 2:] - centre) * y_valid[None, 2:, None]
    update = update + conduct(padded[1:-1, :-2] - centre) * y_valid[None, :-2, None]
    x_flux = conduct(centre[:, :, 1:] - centre[:, :, :-1])
    zero_col = jnp.zeros_like(centre[:, :, :1])
    update = (
        update
        + jnp.concatenate([x_flux, zero_col], axis=2)
        - jnp.concatenate([zero_col, x_flux], axis=2)
    )
    return centre + time_step * update


def shards(projections, angle_index):
    wide_count = lax.axis_size("wide")
    narrow_count = lax.axis_size("narrow")
    per_device = projections.shape[0]
    row_count, col_count = (projections.shape[1], projections.shape[2])
    total_angles = angle_index.shape[0]
    slab_rows = row_count // wide_count
    tile_rows = YV // narrow_count
    wide_pos = lax.axis_index("wide")
    narrow_pos = lax.axis_index("narrow")
    weight_scale = math.pi / total_angles
    kernel = ramp_kernel(col_count)
    thickness = phase_retrieve(projections)
    prepared = apply_ramp(thickness, kernel)
    angle_table = angle_index.reshape(wide_count, narrow_count, per_device)
    own_ids = lax.dynamic_index_in_dim(angle_table, narrow_pos, 1, keepdims=False).reshape(-1)
    own_theta = own_ids.astype(jnp.float32) * weight_scale
    grouped = prepared.reshape(per_device, wide_count, slab_rows, col_count)
    sinogram = lax.all_to_all(grouped, "wide", split_axis=1, concat_axis=0, tiled=True)[:, 0]
    partial_value = back_project(sinogram, own_theta, YV, XV)
    current = (
        lax.psum_scatter(partial_value, "narrow", scatter_dimension=1, tiled=True) * weight_scale
    )
    z_first = wide_pos * slab_rows
    y_first = narrow_pos * tile_rows
    for sweep_index in range(STEPS):
        padded = extended(current, (("wide", 0), ("narrow", 1)), 1)
        current = diffuse_step(padded, z_first - 1, y_first - 1, row_count)
    return current


def solution(mesh):
    return jax.shard_map(
        shards,
        mesh=mesh,
        in_specs=(P(("scan", "wide", "narrow"), None, None), P("scan")),
        out_specs=P(("scan", "wide"), "narrow", None),
        check_vma=False,
    )
```

profile of v0, /device:TPU:0, one launch (start us, length us, event | category | flops | bytes accessed | tf_op | source)
XLA Modules:
  0.0 1616.4 jit_solution(17988574381002744714)
XLA Ops:
  6.5 4.1 fusion.63
  10.7 3.9 fusion.65
  14.5 7.3 fusion.3
  21.8 7.3 convolution_bitcast_fusion.1
  29.1 0.4 fusion.34
  29.5 7.4 convolution_bitcast_fusion
  36.9 0.5 slice_subtract_fusion.4
  37.4 3.6 negate_multiply_fusion
  41.0 3.6 convolution_bitcast_fusion.2
  44.6 7.3 all-to-all-start
  53.2 24.5 %all-to-all-done = f32[1,8,64,512]{3,2,0,1:T(8,128)} async-done(((f32[1,8,64,512]{3,2,0,1:T(8,128)}), f32[1,8,64,512]{3,2,0,1:T(8,128)}, u32[]{:S(2)}, u32[]{:S(2)}) %all-to-all-start) | async-done | bytes 1048608 | tf_op jit(solution)/shard_map/all_to_all | solution.py:174
  77.7 1.8 copy.8
  79.5 703.5 %gather_fusion = f32[65536,64]{1,0:T(8,128)} fusion(f32[8,64,512]{1,2,0:T(8,128)S(1)} %bitcast.88, s32[65536]{0:T(1024)S(1)} %bitcast.90), kind=kCustom, calls=%fused_computation.clone | custom fusion | bytes 34078720 | tf_op jit(solution)/shard_map/while/body/eval_jaxpr/vmap(jit(_take))/gather | solution.py:110
  783.1 703.5 %gather_fusion.1 = f32[65536,64]{1,0:T(8,128)} fusion(f32[8,64,512]{1,2,0:T(8,128)S(1)} %bitcast.89, s32[65536]{0:T(1024)S(1)} %bitcast.91), kind=kCustom, calls=%fused_computation.1.clone | custom fusion | bytes 34078720 | tf_op jit(solution)/shard_map/while/body/eval_jaxpr/vmap(jit(_take))/gather | solution.py:110
  1486.6 44.1 %fusion.1 = f32[64,8192]{0,1:T(8,128)} fusion(f32[8,8192,64]{2,1,0:T(8,128)} %bitcast.93, f32[8,8192,64]{2,1,0:T(8,128)} %bitcast.92, f32[8,8192]{1,0:T(8,128)S(1)} %get-tuple-element.52, f32[8,8192]{1,0:T(8,128)S(1)} %get-tuple-element.51, pred[8,8192]{1,0:T(8,128)(4,1)S(1)} %get-tuple-element.50, pred[8,8192]{1,0:T(8,128)(4,1)S(1)} %get-tuple-element.49), kind=kLoop, calls=%fused_computation.4 | loop fusion | flops 24641536 | bytes 36306944 | tf_op jit(solution)/shard_map/while/body/eval_jaxpr/reduce_sum | solution.py:125
  1530.6 4.2 copy.9
  1535.0 8.7 reduce-scatter.2.cloned.1.call-done
  1543.6 1.3 broadcast_multiply_fusion
  1545.0 1.3 collective-permute-start
  1546.3 4.5 collective-permute-start.1
  1550.9 1.3 collective-permute-done.1
  1552.3 1.3 collective-permute-start.2
  1553.6 3.0 collective-permute-start.3
  1556.7 0.3 add_divide_fusion.3
  1557.0 0.5 collective-permute-done.3
  1557.5 2.5 multiply_add_fusion.3
  1560.1 1.3 collective-permute-start.4
  1561.4 5.2 collective-permute-start.5
  1566.6 1.4 collective-permute-done.5
  1568.0 1.3 collective-permute-start.6
  1569.3 3.0 collective-permute-start.7
  1572.4 0.3 add_divide_fusion.2
  1572.7 0.5 collective-permute-done.7
  1573.2 2.6 multiply_add_fusion.2
  1575.8 1.3 collective-permute-start.8
  1577.1 5.7 collective-permute-start.9
  1582.8 1.4 collective-permute-done.9
  1584.3 1.3 collective-permute-start.10
  1585.6 3.0 collective-permute-start.11
  1589.0 0.5 collective-permute-done.11
  1589.5 2.6 multiply_add_fusion.1
  1592.1 1.3 collective-permute-start.12
  1593.4 5.7 collective-permute-start.13
  1599.1 1.4 collective-permute-done.13
  1600.6 1.3 collective-permute-start.14
  1601.9 3.0 collective-permute-start.15
  1605.3 0.5 collective-permute-done.15
  1605.8 3.4 multiply_add_fusion
  (42 shorter events, 2.5 us)
Async XLA Ops:
  6.5 8.0 copy-start
  37.4 14.5 copy-start.2
  44.6 33.1 %all-to-all-start = ((f32[1,8,64,512]{3,2,0,1:T(8,128)}), f32[1,8,64,512]{3,2,0,1:T(8,128)}, u32[]{:S(2)}, u32[]{:S(2)}) async-start(f32[1,8,64,512]{3,2,0,1:T(8,128)} %convolution_bitcast_fusion.2), calls=%async_computation | async-start | bytes 2097152 | tf_op jit(solution)/shard_map/all_to_all | solution.py:174
  51.8 1491.8 %reduce-scatter.2.cloned.1.call-start = ((), (), s32[]{:S(2)}) async-start(), calls=%async_computation.2 | async-start | bytes 3145728 | tf_op jit(solution)/shard_map/reduce_scatter | solution.py:177
  1545.0 5.9 collective-permute-start
  1546.3 6.0 collective-permute-start.1
  1552.3 4.7 collective-permute-start.2
  1553.6 3.9 collective-permute-start.3
  1560.1 6.5 collective-permute-start.4
  1561.4 6.6 collective-permute-start.5
  1568.0 4.7 collective-permute-start.6
  1569.3 3.9 collective-permute-start.7
  1573.2 35.9 %copy-start.1 = (f32[1,512,512]{2,1,0:T(8,128)S(1)}, f32[1,512,512]{2,1,0:T(8,128)}, u32[]{:S(2)}) copy-start(f32[1,512,512]{2,1,0:T(8,128)} %param.4) | copy-start | bytes 3145732
  1575.8 7.0 collective-permute-start.8
  1577.1 7.2 collective-permute-start.9
  1584.3 4.7 collective-permute-start.10
  1585.6 3.9 collective-permute-start.11
  1592.1 7.0 collective-permute-start.12
  1593.4 7.2 collective-permute-start.13
  1600.6 4.7 collective-permute-start.14
  1601.9 3.9 collective-permute-start.15
Sparse Core Ops, SparseCore 0:
  1535.0 8.6 reduce-scatter.1
where the time goes:
time: 1630 us; the launch traced here: 1620 us
  local copies, waits for them, and re-layouts  1410 us (87%)
  other arithmetic  68 us (4%)
  starting transfers between devices  50.9 us (3%)
  waiting for transfers between devices  40.7 us (2%)
  matrix products  29.1 us (2%)
    gather x1, local copies, waits for them, and re-layouts, one_angle(): jnp.take(row_data, index_row, axis=1)  704 us
    gather x1, local copies, waits for them, and re-layouts, one_angle(): jnp.take(row_data, index_row + 1, axis=1)  703 us
    reduce_sum x1, other arithmetic, add_block(): return accum_sum + jnp.sum(values, axis=0).reshape(slices, y_count, x_width)  44.1 us
    ppermute x8, starting transfers between devices, extended(): lax.ppermute(tail, axis, [(i, (i + 1) % count) for i in range(ends)])  33.3 us
  transfers between devices with their start and end apart: 18, of which 10 were waited for; matrix products, arithmetic and copies ran while one was open for 0% of the time, Pallas kernels for 0%

commit v1 on v0

v1 whole, which is shorter than its diff:
```python
import functools
import math

import jax
import jax.numpy as jnp
import ml_dtypes
import numpy as np
from jax import lax
from jax.experimental import pallas as pl
from jax.experimental.pallas import tpu as pltpu
from jax.sharding import PartitionSpec as P

XV = 128
YV = 64
STEPS = 4
GROUP = 16
MAIN = 128
SIDE = 8

paganin_strength = 0.25
attenuation = 0.01
contrast = 0.8
time_step = 0.15
bf16 = jnp.bfloat16
f32 = jnp.float32


def halves(table):
    high = table.astype(ml_dtypes.bfloat16)
    low = (table - high.astype(np.float64)).astype(ml_dtypes.bfloat16)
    return high, low


def hartley_table(count):
    grid = np.arange(count)
    phase = (grid[:, None] * grid[None, :] % count) * (2.0 * math.pi / count)
    return (np.cos(phase) + np.sin(phase)) / math.sqrt(count)


def window_columns(col_count):
    first = col_count // 2 - MAIN // 2
    middle = np.arange(first, first + MAIN)
    before = np.arange(first - SIDE, first)
    after = np.arange(first + MAIN, first + MAIN + SIDE)
    return np.concatenate([middle, before, after])


def ramp_table(col_count, scale):
    grid = np.arange(col_count)
    columns = window_columns(col_count)
    offset = grid[:, None] - columns[None, :]
    odd = offset % 2 != 0
    safe = np.where(odd, offset, 1)
    table = np.where(offset == 0, 0.25, np.where(odd, -1.0 / (math.pi * safe) ** 2, 0.0)) * scale
    return np.pad(table, ((0, 0), (0, 2 * MAIN - columns.size)))


def split(value):
    high = value.astype(bf16)
    return high, (value - high.astype(f32)).astype(bf16)


def dot3(left, right):
    dot = functools.partial(jnp.dot, preferred_element_type=f32)
    return dot(left[0], right[0]) + (dot(left[0], right[1]) + dot(left[1], right[0]))


def filter_kernel(x_ref, hh_ref, hl_ref, kh_ref, kl_ref, row_ref, col_ref, out_ref, ah, al, bh, bl):
    rows, cols = x_ref.shape
    block = 128

    def columns_first(step, carry):
        own = pl.ds(pl.multiple_of(step * block, block), block)
        part = dot3(split(x_ref[own, :]), (hh_ref[...], hl_ref[...]))
        ah[own, :], al[own, :] = split(part)
        return carry

    def damp(step, carry):
        own = pl.ds(pl.multiple_of(step * block, block), block)
        part = dot3((hh_ref[own, :], hl_ref[own, :]), (ah[...], al[...]))
        part = part / (row_ref[own, :] + col_ref[...])
        part = dot3(split(part), (hh_ref[...], hl_ref[...]))
        bh[own, :], bl[own, :] = split(part)
        return carry

    def ramp(step, carry):
        own = pl.ds(pl.multiple_of(step * block, block), block)
        part = dot3((hh_ref[own, :], hl_ref[own, :]), (bh[...], bl[...]))
        out_ref[own, :] = dot3(split(jnp.log(part)), (kh_ref[...], kl_ref[...]))
        return carry

    lax.fori_loop(0, rows // block, columns_first, 0)
    lax.fori_loop(0, rows // block, damp, 0)
    lax.fori_loop(0, rows // block, ramp, 0)


def filtered_window(projection, total_angles):
    rows, cols = projection.shape
    tables = halves(hartley_table(rows)) + halves(
        ramp_table(cols, -math.pi / (attenuation * total_angles))
    )
    row_part = 1.0 + paganin_strength * 4.0 * np.sin(np.pi * np.arange(rows) / rows) ** 2
    col_part = paganin_strength * 4.0 * np.sin(np.pi * np.arange(cols) / cols) ** 2
    vmem = pl.BlockSpec(memory_space=pltpu.VMEM)
    return pl.pallas_call(
        filter_kernel,
        out_shape=jax.ShapeDtypeStruct((rows, 2 * MAIN), f32),
        in_specs=[vmem] * 7,
        out_specs=vmem,
        scratch_shapes=[pltpu.VMEM((rows, cols), bf16)] * 4,
        compiler_params=pltpu.CompilerParams(vmem_limit_bytes=48 * 2**20),
        name="filter_window",
    )(
        projection,
        *[jnp.asarray(table) for table in tables],
        jnp.asarray(row_part[:, None].astype(np.float32)),
        jnp.asarray(col_part[None, :].astype(np.float32)),
    )


def conduct(diff):
    base = 1.0 + diff * diff * (1.0 / contrast**2)
    guess = pl.reciprocal(base, approx=True)
    return diff * (guess * (2.0 - base * guess))


def volume_kernel(plan, ang_ref, cos_ref, sin_ref, sino_ref, out_ref, f2, wh0, wl0, wh1, wl1, u):
    slab, tile_y, local_y, z_start, wide_count = plan
    total, depth = sino_ref.shape[0], sino_ref.shape[1]
    wide_pos, narrow_pos = lax.axis_index("wide"), lax.axis_index("narrow")
    y_skip = tile_y - (local_y - tile_y)
    y_first = narrow_pos * y_skip
    x_row = lax.broadcasted_iota(jnp.int32, (16, XV), 1).astype(f32) + (0.5 - 0.5 * XV)
    lanes16 = lax.broadcasted_iota(jnp.int32, (16, XV), 0)
    middle = [(lanes16 + (SIDE + 16 * j)).astype(f32).astype(bf16) for j in range(MAIN // 16)]
    outer = jnp.where(lanes16 < SIDE, lanes16, lanes16 + MAIN).astype(f32).astype(bf16)
    cells = middle + [outer]
    centre = 0.5 * MAIN + SIDE - 0.5

    def weights(group, pair, high_ref, low_ref):
        for side in range(2):
            own = slice(side * XV, (side + 1) * XV)
            y_pos = (y_first + 2 * pair + side).astype(f32) + (0.5 - 0.5 * YV)
            for a in range(GROUP):
                number = ang_ref[group * GROUP + a]
                place = x_row * cos_ref[number] + (y_pos * sin_ref[number] + centre)
                lower = jnp.floor(place)
                frac = place - lower
                coarse = jnp.floor(frac * 256.0 + 0.5) * (1.0 / 256.0)
                fine = frac - coarse
                here, there = lower.astype(bf16), (lower + 1.0).astype(bf16)
                left, right = (1.0 - coarse).astype(bf16), coarse.astype(bf16)
                left_fine, right_fine = (-fine).astype(bf16), fine.astype(bf16)
                zero = jnp.zeros_like(left)
                for j, cell in enumerate(cells):
                    row = a * MAIN + j * 16 if j < len(middle) else GROUP * MAIN + a * 16
                    is_here, is_there = cell == here, cell == there
                    high_ref[row : row + 16, own] = jnp.where(
                        is_here, left, jnp.where(is_there, right, zero)
                    )
                    low_ref[row : row + 16, own] = jnp.where(
                        is_here, left_fine, jnp.where(is_there, right_fine, zero)
                    )

    def project(group, pair, high_ref, low_ref):
        both = jnp.dot(f2[...], high_ref[...], preferred_element_type=f32)
        rest = jnp.dot(f2[:depth, :], low_ref[...], preferred_element_type=f32)
        value = both[:depth] + (both[depth:] + rest)
        for side in range(2):
            own = value[:, side * XV : (side + 1) * XV]
            if total > GROUP:
                own = own + jnp.where(group > 0, u[2 * pair + side], 0.0)
            u[2 * pair + side] = own

    def one_group(group, carry):
        for a in range(GROUP):
            high, low = split(sino_ref[group * GROUP + a])
            f2[:depth, a * MAIN : (a + 1) * MAIN] = high[:, :MAIN]
            f2[depth:, a * MAIN : (a + 1) * MAIN] = low[:, :MAIN]
        for half in range(2):
            parts = [
                sino_ref[group * GROUP + half * 8 + a][:, MAIN : MAIN + 2 * SIDE] for a in range(8)
            ]
            high, low = split(jnp.concatenate(parts, axis=1))
            own = slice(GROUP * MAIN + half * MAIN, GROUP * MAIN + (half + 1) * MAIN)
            f2[:depth, own] = high
            f2[depth:, own] = low
        weights(group, jnp.int32(0), wh0, wl0)

        def two_pairs(step, inner):
            weights(group, 2 * step + 1, wh1, wl1)
            project(group, 2 * step, wh0, wl0)
            weights(group, 2 * step + 2, wh0, wl0)
            project(group, 2 * step + 1, wh1, wl1)
            return inner

        lax.fori_loop(0, local_y // 4, two_pairs, 0)
        return carry

    if total > GROUP:
        lax.fori_loop(0, total // GROUP, one_group, 0)
    else:
        one_group(0, 0)

    z_ids = lax.broadcasted_iota(jnp.int32, (depth, XV), 0)
    x_ids = lax.broadcasted_iota(jnp.int32, (depth, XV), 1)
    has_z = z_ids < depth - 1
    has_x = x_ids < XV - 1

    def row_step(y, carry):
        now, flux_before = carry
        later = u[jnp.minimum(y + 1, local_y - 1)]
        flux_y = conduct(later - now)
        flux_z = conduct(jnp.where(has_z, pltpu.roll(now, depth - 1, 0) - now, 0.0))
        flux_x = conduct(jnp.where(has_x, pltpu.roll(now, XV - 1, 1) - now, 0.0))
        update = (flux_y - flux_before) + (flux_z - pltpu.roll(flux_z, 1, 0))
        update = update + (flux_x - pltpu.roll(flux_x, 1, 1))
        u[y] = now + time_step * update
        return later, flux_y

    for step in range(STEPS):
        lax.fori_loop(0, local_y, row_step, (u[0], jnp.zeros((depth, XV), f32)), unroll=2)

    z_skip = wide_pos * slab - z_start(wide_pos)
    if slab % 8 == 0:
        z_skip = pl.multiple_of(z_skip, 8)
    y_own = narrow_pos * (local_y - tile_y)
    for y in range(tile_y):
        out_ref[:, y, :] = u[y_own + y, pl.ds(z_skip, slab), :]


def shards(projections, angle_index):
    wide_count = lax.axis_size("wide")
    narrow_count = lax.axis_size("narrow")
    rows = projections.shape[1]
    per_device = projections.shape[0]
    total = angle_index.shape[0]
    slab = rows // wide_count
    depth = -(-(slab + 12) // 16) * 16
    tile_y = YV // narrow_count
    local_y = tile_y + STEPS

    def z_start(wide_pos):
        first = (wide_pos * slab + 8 - STEPS) // 8 * 8 - 8
        if isinstance(wide_pos, int):
            return min(max(first, 0), rows - depth)
        return jnp.minimum(jnp.maximum(first, 0), rows - depth)

    windows = [filtered_window(projections[i], total) for i in range(per_device)]
    window = jnp.stack(windows)
    slabs = jnp.stack(
        [window[:, z_start(w) : z_start(w) + depth] for w in range(wide_count) for n in range(narrow_count)]
    )
    sino = lax.all_to_all(slabs, ("wide", "narrow"), split_axis=0, concat_axis=0, tiled=True)
    sino = sino.reshape(total, depth, 2 * MAIN)
    angles = np.arange(total) * (math.pi / total)
    vmem = pl.BlockSpec(memory_space=pltpu.VMEM)
    smem = pl.BlockSpec(memory_space=pltpu.SMEM)
    inner = GROUP * (MAIN + 2 * SIDE)
    return pl.pallas_call(
        functools.partial(volume_kernel, (slab, tile_y, local_y, z_start, wide_count)),
        out_shape=jax.ShapeDtypeStruct((slab, tile_y, XV), f32),
        in_specs=[smem, smem, smem, vmem],
        out_specs=vmem,
        scratch_shapes=[pltpu.VMEM((2 * depth, inner), bf16)]
        + [pltpu.VMEM((inner, 2 * XV), bf16)] * 4
        + [pltpu.VMEM((local_y, depth, XV), f32)],
        compiler_params=pltpu.CompilerParams(vmem_limit_bytes=48 * 2**20),
        name="volume",
    )(
        angle_index,
        jnp.asarray(np.cos(angles).astype(np.float32)),
        jnp.asarray(np.sin(angles).astype(np.float32)),
        sino,
    )


def solution(mesh):
    return jax.shard_map(
        shards,
        mesh=mesh,
        in_specs=(P(("scan", "wide", "narrow"), None, None), P("scan")),
        out_specs=P(("scan", "wide"), "narrow", None),
        check_vma=False,
    )
```

time: 1630 us -> 86.1 us (0.05)
  local copies, waits for them, and re-layouts: 1410 us -> 6.99 us
  other arithmetic: 68 us -> 0 us
  starting transfers between devices: 50.9 us -> 0 us
  waiting for transfers between devices: 40.7 us -> 0 us
  Pallas kernels: 0 us -> 39.4 us
  blocking collectives: 0 us -> 38.8 us
  matrix products: 29.1 us -> 0 us
    gather x2 -> x0, local copies, waits for them, and re-layouts: 1410 us -> none  [the longest x1 704 us: one_angle(): jnp.take(row_data, index_row, axis=1)]
    reduce_sum x1 -> x0, other arithmetic: 44.1 us -> none  [add_block(): return accum_sum + jnp.sum(values, axis=0).reshape(slices, y_count, x_width)]
    ppermute x16 -> x0, starting transfers between devices: 43.6 us -> none  [the longest x8 33.3 us: extended(): lax.ppermute(tail, axis, [(i, (i + 1) % count) for i in range(ends)])]
    pallas_call x0 -> x2, Pallas kernels: none -> 39.4 us  [the longest x1 32.1 us: shards(): pl.pallas_call(functools.partial(volume_kernel, (slab, tile_y, local_y, z...]
    all_to_all x0 -> x1, blocking collectives: none -> 38.8 us  [shards(): lax.all_to_all(slabs, ('wide', 'narrow'), split_axis=0, concat_axis=0, ti...]
    dot_general x5 -> x0, matrix products: 29.1 us -> none  [the longest x1 7.43 us: phase_retrieve(): jnp.einsum('mr,ard->amd', row_pair, spectrum, precision=highest, preferre...]
    all_to_all x1 -> x0, waiting for transfers between devices: 24.5 us -> none  [shards(): lax.all_to_all(grouped, 'wide', split_axis=1, concat_axis=0, tiled=True)]
  transfers between devices with their start and end apart: 18 -> 0, of which waited for: 10 -> 0; matrix products, arithmetic and copies ran while one was open for 0% -> 0% of each run, Pallas kernels for 0% -> 0%
where the time goes in v1:
time: 86.1 us; the launch traced here: 85.4 us
  Pallas kernels  39.4 us (46%)
  blocking collectives  38.8 us (45%)
  local copies, waits for them, and re-layouts  6.99 us (8%)
    all_to_all x1, blocking collectives, shards(): lax.all_to_all(slabs, ('wide', 'narrow'), split_axis=0, concat_axis=0, ti...  38.8 us
    pallas_call x1, Pallas kernels, shards(): pl.pallas_call(functools.partial(volume_kernel, (slab, tile_y, local_y, z...  32.1 us
    pallas_call x1, Pallas kernels, filtered_window(): pl.pallas_call(filter_kernel, out_shape=jax.ShapeDtypeStruct((rows, 2 * M...  7.31 us
    unnamed x35, local copies, waits for them, and re-layouts  6.98 us

profile of v1, /device:TPU:0, one launch (start us, length us, event | category | flops | bytes accessed | tf_op | source)
XLA Modules:
  0.0 85.4 jit_solution(7437977214820074202)
XLA Ops:
  0.0 0.0 copy-start
  0.0 1.2 %copy-done = f32[1,512,512]{2,1,0:T(8,128)S(1)} copy-done((f32[1,512,512]{2,1,0:T(8,128)S(1)}, f32[1,512,512]{2,1,0:T(8,128)}, u32[]{:S(2)}) %copy-start) | copy-done | bytes 1048600
  1.2 0.0 copy-start.1
  1.2 1.0 %copy-done.1 = bf16[512,512]{1,0:T(8,128)(2,1)S(1)} copy-done((bf16[512,512]{1,0:T(8,128)(2,1)S(1)}, bf16[512,512]{1,0:T(8,128)(2,1)}, u32[]{:S(2)}) %copy-start.1) | copy-done | bytes 524312
  2.3 0.0 copy-start.2
  2.3 1.0 %copy-done.2 = bf16[512,512]{1,0:T(8,128)(2,1)S(1)} copy-done((bf16[512,512]{1,0:T(8,128)(2,1)S(1)}, bf16[512,512]{1,0:T(8,128)(2,1)}, u32[]{:S(2)}) %copy-start.2) | copy-done | bytes 524312
  3.3 0.0 copy-start.3
  3.3 0.9 %copy-done.3 = f32[512,1]{1,0:T(8,128)S(1)} copy-done((f32[512,1]{1,0:T(8,128)S(1)}, f32[512,1]{1,0:T(8,128)}, u32[]{:S(2)}) %copy-start.3) | copy-done | bytes 2072
  4.3 0.0 copy-start.4
  4.3 0.9 %copy-done.4 = bf16[512,256]{1,0:T(8,128)(2,1)S(1)} copy-done((bf16[512,256]{1,0:T(8,128)(2,1)S(1)}, bf16[512,256]{1,0:T(8,128)(2,1)}, u32[]{:S(2)}) %copy-start.4) | copy-done | bytes 262168
  5.2 0.0 copy-start.5
  5.2 0.9 %copy-done.5 = bf16[512,256]{1,0:T(8,128)(2,1)S(1)} copy-done((bf16[512,256]{1,0:T(8,128)(2,1)S(1)}, bf16[512,256]{1,0:T(8,128)(2,1)}, u32[]{:S(2)}) %copy-start.5) | copy-done | bytes 262168
  6.2 0.0 copy-start.6
  6.2 0.7 copy-done.6
  6.8 7.3 %filter_window.1 = f32[512,256]{1,0:T(8,128)S(1)} custom-call(f32[512,512]{1,0:T(8,128)S(1)} %bitcast.68, bf16[512,512]{1,0:T(8,128)(2,1)S(1)} %copy-done.2, bf16[512,512]{1,0:T(8,128)(2,1)S(1)} %copy-done.1, bf16[512,256]{1,0:T(8,128)(2,1)S(1)} %copy-done.5, bf16[512,256]{1,0:T(8,128)(2,1)S(1)} %copy-done.4, f32[512,1]{1,0:T(8,128)S(1)} %copy-done.3, ...), custom_call_target="tpu_custom_call" | custom-call | tf_op jit(solution)/shard_map/filter_window/pallas_call | solution.py:105
  14.4 0.0 copy-start.7
  14.4 0.0 copy-start.8
  14.4 0.0 copy-start.9
  14.5 38.8 %all_to_all.5 = f32[16,1,80,256]{3,2,1,0:T(8,128)S(1)} all-to-all(f32[16,1,80,256]{3,2,1,0:T(8,128)S(1)} %fusion.15), channel_id=1, replica_groups=mesh['scan'=2,'wide'=8,'narrow'=2] {'wide','narrow'}, dimensions={0} | all-to-all | bytes 2621440 | tf_op jit(solution)/shard_map/all_to_all | solution.py:254
  53.3 0.0 copy-done.7
  53.3 0.0 copy-done.8
  53.3 0.0 copy-done.9
  53.3 32.1 %volume.1 = f32[64,32,128]{2,1,0:T(8,128)} custom-call(s32[16]{0:T(128)S(1)} %copy-done.7, f32[16]{0:T(128)S(1)} %copy-done.9, f32[16]{0:T(128)S(1)} %copy-done.8, f32[16,80,256]{2,1,0:T(8,128)S(1)} %bitcast.67), custom_call_target="tpu_custom_call" | custom-call | tf_op jit(solution)/shard_map/volume/pallas_call | solution.py:260
  (16 shorter events, 0.1 us)
Async XLA Ops:
  0.0 1.2 %copy-start = (f32[1,512,512]{2,1,0:T(8,128)S(1)}, f32[1,512,512]{2,1,0:T(8,128)}, u32[]{:S(2)}) copy-start(f32[1,512,512]{2,1,0:T(8,128)} %param.10) | copy-start | bytes 3145732
  1.2 1.0 %copy-start.1 = (bf16[512,512]{1,0:T(8,128)(2,1)S(1)}, bf16[512,512]{1,0:T(8,128)(2,1)}, u32[]{:S(2)}) copy-start(bf16[512,512]{1,0:T(8,128)(2,1)} %constant.17.clone.hl_ref) | copy-start | bytes 1572868
  2.3 1.0 %copy-start.2 = (bf16[512,512]{1,0:T(8,128)(2,1)S(1)}, bf16[512,512]{1,0:T(8,128)(2,1)}, u32[]{:S(2)}) copy-start(bf16[512,512]{1,0:T(8,128)(2,1)} %constant.16.clone.hh_ref) | copy-start | bytes 1572868
  3.3 0.9 %copy-start.3 = (f32[512,1]{1,0:T(8,128)S(1)}, f32[512,1]{1,0:T(8,128)}, u32[]{:S(2)}) copy-start(f32[512,1]{1,0:T(8,128)} %constant.20.clone.row_ref) | copy-start | bytes 6148
  4.3 0.9 %copy-start.4 = (bf16[512,256]{1,0:T(8,128)(2,1)S(1)}, bf16[512,256]{1,0:T(8,128)(2,1)}, u32[]{:S(2)}) copy-start(bf16[512,256]{1,0:T(8,128)(2,1)} %constant.19.clone.kl_ref) | copy-start | bytes 786436
  5.2 0.9 %copy-start.5 = (bf16[512,256]{1,0:T(8,128)(2,1)S(1)}, bf16[512,256]{1,0:T(8,128)(2,1)}, u32[]{:S(2)}) copy-start(bf16[512,256]{1,0:T(8,128)(2,1)} %constant.18.clone.kh_ref) | copy-start | bytes 786436
  6.2 0.7 copy-start.6
  14.4 38.8 %copy-start.7 = (s32[16]{0:T(128)S(1)}, s32[16]{0:T(128)}, u32[]{:S(2)}) copy-start(s32[16]{0:T(128)} %ang_ref.1) | copy-start | bytes 196
  14.4 38.8 %copy-start.8 = (f32[16]{0:T(128)S(1)}, f32[16]{0:T(128)}, u32[]{:S(2)}) copy-start(f32[16]{0:T(128)} %constant.23.clone.sin_ref) | copy-start | bytes 196
  14.4 38.8 %copy-start.9 = (f32[16]{0:T(128)S(1)}, f32[16]{0:T(128)}, u32[]{:S(2)}) copy-start(f32[16]{0:T(128)} %constant.22.clone.cos_ref) | copy-start | bytes 196

commit v2 on v1

--- a/solution.py
+++ b/solution.py
@@ -65,56 +65,187 @@
     return dot(left[0], right[0]) + (dot(left[0], right[1]) + dot(left[1], right[0]))
 
 
-def filter_kernel(x_ref, hh_ref, hl_ref, kh_ref, kl_ref, row_ref, col_ref, out_ref, ah, al, bh, bl):
-    rows, cols = x_ref.shape
+def each(start, stop, body):
+    if stop - start <= 16:
+        for i in range(start, stop):
+            body(i)
+    else:
+
+        def step(i, carry):
+            body(i)
+            return carry
+
+        lax.fori_loop(start, stop, step, 0)
+
+
+def exchange_kernel(
+    plan, x_any, h_any, k_any, row_any, col_any, sino, x, h, k, row, col, ah, al, bh, bl, window,
+    pack, load_sem, own_sem, send_sem, recv_sem, pass_sem, land_sem,
+):
+    wide_count, depth, starts = plan
+    rows = x.shape[0]
     block = 128
+    mesh_ids = pl.DeviceIdType.MESH
+    wide_pos, narrow_pos = lax.axis_index("wide"), lax.axis_index("narrow")
+    other = 1 - narrow_pos
+    moves = ((h_any, h), (x_any.at[0], x), (row_any, row), (col_any, col), (k_any, k))
+    loads = [
+        pltpu.make_async_copy(source, target, load_sem.at[i])
+        for i, (source, target) in enumerate(moves)
+    ]
+    for load in loads:
+        load.start()
+
+    def greet(offset):
+        target = lax.rem(wide_pos + offset, wide_count)
+        pl.semaphore_signal(barrier, inc=1, device_id={"wide": target}, device_id_type=mesh_ids)
+
+    barrier = pltpu.get_barrier_semaphore()
+    each(1, wide_count, greet)
+    pl.semaphore_signal(barrier, inc=1, device_id={"narrow": other}, device_id_type=mesh_ids)
+
+    def part_of(step):
+        return pl.ds(pl.multiple_of(step * block, block), block)
 
     def columns_first(step, carry):
-        own = pl.ds(pl.multiple_of(step * block, block), block)
-        part = dot3(split(x_ref[own, :]), (hh_ref[...], hl_ref[...]))
-        ah[own, :], al[own, :] = split(part)
+        own = part_of(step)
+        ah[own, :], al[own, :] = split(dot3(split(x[own, :]), (h[0], h[1])))
         return carry
 
     def damp(step, carry):
-        own = pl.ds(pl.multiple_of(step * block, block), block)
-        part = dot3((hh_ref[own, :], hl_ref[own, :]), (ah[...], al[...]))
-        part = part / (row_ref[own, :] + col_ref[...])
-        part = dot3(split(part), (hh_ref[...], hl_ref[...]))
-        bh[own, :], bl[own, :] = split(part)
+        own = part_of(step)
+        part = dot3((h[0, own, :], h[1, own, :]), (ah[...], al[...]))
+        part = part / (jnp.concatenate([row[own, :]] * (part.shape[1] // 128), axis=1) + col[...])
+        bh[own, :], bl[own, :] = split(dot3(split(part), (h[0], h[1])))
         return carry
 
     def ramp(step, carry):
-        own = pl.ds(pl.multiple_of(step * block, block), block)
-        part = dot3((hh_ref[own, :], hl_ref[own, :]), (bh[...], bl[...]))
-        out_ref[own, :] = dot3(split(jnp.log(part)), (kh_ref[...], kl_ref[...]))
+        own = part_of(step)
+        part = dot3((h[0, own, :], h[1, own, :]), (bh[...], bl[...]))
+        window[own, :] = dot3(split(jnp.log(part)), (k[0], k[1]))
         return carry
 
+    loads[0].wait()
+    loads[1].wait()
     lax.fori_loop(0, rows // block, columns_first, 0)
+    for load in loads[2:]:
+        load.wait()
     lax.fori_loop(0, rows // block, damp, 0)
     lax.fori_loop(0, rows // block, ramp, 0)
-
-
-def filtered_window(projection, total_angles):
-    rows, cols = projection.shape
-    tables = halves(hartley_table(rows)) + halves(
-        ramp_table(cols, -math.pi / (attenuation * total_angles))
+    for w, start in enumerate(starts):
+        pack[w, :depth, :] = window[start : start + depth, :MAIN]
+        sides = [
+            window[start + 16 * j : start + 16 * j + 16, MAIN : MAIN + 2 * SIDE]
+            for j in range(depth // 16)
+        ]
+        pack[w, depth:, : depth] = jnp.concatenate(sides, axis=1)
+        pack[w, depth:, depth:] = jnp.zeros((16, MAIN - depth), f32)
+
+    pl.semaphore_wait(barrier, wide_count)
+
+    def offset_of(turn):
+        return 1 + (turn + wide_count // 2 - 1) % (wide_count - 1)
+
+    def send(turn):
+        offset = offset_of(turn)
+        target = lax.rem(wide_pos + offset, wide_count)
+        pltpu.make_async_remote_copy(
+            src_ref=pack.at[target],
+            dst_ref=sino.at[wide_pos * 2 + narrow_pos],
+            send_sem=send_sem.at[offset],
+            recv_sem=recv_sem.at[offset],
+            device_id={"wide": target},
+            device_id_type=mesh_ids,
+        ).start()
+
+    def arrival(offset):
+        source = lax.rem(wide_pos + wide_count - offset, wide_count)
+        target = lax.rem(wide_pos + offset, wide_count)
+        return pltpu.make_async_remote_copy(
+            src_ref=pack.at[target],
+            dst_ref=sino.at[source * 2 + narrow_pos],
+            send_sem=send_sem.at[offset],
+            recv_sem=recv_sem.at[offset],
+            device_id={"wide": target},
+            device_id_type=mesh_ids,
+        )
+
+    def hand_on(offset, side):
+        source = lax.rem(wide_pos + wide_count - offset, wide_count)
+        return pltpu.make_async_remote_copy(
+            src_ref=sino.at[source * 2 + narrow_pos],
+            dst_ref=sino.at[source * 2 + side],
+            send_sem=pass_sem.at[offset],
+            recv_sem=land_sem.at[offset],
+            device_id={"narrow": other},
+            device_id_type=mesh_ids,
+        )
+
+    each(0, wide_count - 1, send)
+    own_copy = pltpu.make_async_copy(
+        pack.at[wide_pos], sino.at[wide_pos * 2 + narrow_pos], own_sem
     )
+    own_copy.start()
+    own_copy.wait()
+    hand_on(0, narrow_pos).start()
+
+    def forward(turn):
+        offset = offset_of(wide_count - 2 - turn)
+        arrival(offset).wait_recv()
+        hand_on(offset, narrow_pos).start()
+
+    def finish(turn):
+        offset = offset_of(wide_count - 2 - turn)
+        arrival(offset).wait_send()
+        hand_on(offset, narrow_pos).wait_send()
+        hand_on(offset, other).wait_recv()
+
+    each(0, wide_count - 1, forward)
+    hand_on(0, narrow_pos).wait_send()
+    hand_on(0, other).wait_recv()
+    each(0, wide_count - 1, finish)
+
+
+def exchanged(projection, total, wide_count, depth, starts):
+    rows, cols = projection.shape[1:]
+    hartley = np.stack(halves(hartley_table(rows)))
+    ramp = np.stack(halves(ramp_table(cols, -math.pi / (attenuation * total))))
     row_part = 1.0 + paganin_strength * 4.0 * np.sin(np.pi * np.arange(rows) / rows) ** 2
     col_part = paganin_strength * 4.0 * np.sin(np.pi * np.arange(cols) / cols) ** 2
-    vmem = pl.BlockSpec(memory_space=pltpu.VMEM)
+    row_part = np.repeat(row_part[:, None].astype(np.float32), 128, axis=1)
+    col_part = col_part[None, :].astype(np.float32)
+    anywhere = pl.BlockSpec(memory_space=pl.ANY)
+    dma = pltpu.SemaphoreType.DMA
     return pl.pallas_call(
-        filter_kernel,
-        out_shape=jax.ShapeDtypeStruct((rows, 2 * MAIN), f32),
-        in_specs=[vmem] * 7,
-        out_specs=vmem,
-        scratch_shapes=[pltpu.VMEM((rows, cols), bf16)] * 4,
-        compiler_params=pltpu.CompilerParams(vmem_limit_bytes=48 * 2**20),
-        name="filter_window",
+        functools.partial(exchange_kernel, (wide_count, depth, starts)),
+        out_shape=jax.ShapeDtypeStruct((total, depth + 16, MAIN), f32),
+        in_specs=[anywhere] * 5,
+        out_specs=pl.BlockSpec(memory_space=pltpu.VMEM),
+        scratch_shapes=[
+            pltpu.VMEM((rows, cols), f32),
+            pltpu.VMEM(hartley.shape, bf16),
+            pltpu.VMEM(ramp.shape, bf16),
+            pltpu.VMEM(row_part.shape, f32),
+            pltpu.VMEM(col_part.shape, f32),
+        ]
+        + [pltpu.VMEM((rows, cols), bf16)] * 4
+        + [
+            pltpu.VMEM((rows, 2 * MAIN), f32),
+            pltpu.VMEM((wide_count, depth + 16, MAIN), f32),
+            dma((5,)),
+            dma,
+        ]
+        + [dma((wide_count,))] * 4,
+        compiler_params=pltpu.CompilerParams(
+            vmem_limit_bytes=60 * 2**20, collective_id=0, has_side_effects=True
+        ),
+        name="filter_exchange",
     )(
         projection,
-        *[jnp.asarray(table) for table in tables],
-        jnp.asarray(row_part[:, None].astype(np.float32)),
-        jnp.asarray(col_part[None, :].astype(np.float32)),
+        jnp.asarray(hartley),
+        jnp.asarray(ramp),
+        jnp.asarray(row_part),
+        jnp.asarray(col_part),
     )
 
 
@@ -126,7 +257,7 @@
 
 def volume_kernel(plan, ang_ref, cos_ref, sin_ref, sino_ref, out_ref, f2, wh0, wl0, wh1, wl1, u):
     slab, tile_y, local_y, z_start, wide_count = plan
-    total, depth = sino_ref.shape[0], sino_ref.shape[1]
+    total, depth = sino_ref.shape[0], sino_ref.shape[1] - 16
     wide_pos, narrow_pos = lax.axis_index("wide"), lax.axis_index("narrow")
     y_skip = tile_y - (local_y - tile_y)
     y_first = narrow_pos * y_skip
@@ -174,17 +305,16 @@
 
     def one_group(group, carry):
         for a in range(GROUP):
-            high, low = split(sino_ref[group * GROUP + a])
-            f2[:depth, a * MAIN : (a + 1) * MAIN] = high[:, :MAIN]
-            f2[depth:, a * MAIN : (a + 1) * MAIN] = low[:, :MAIN]
-        for half in range(2):
+            high, low = split(sino_ref[group * GROUP + a, :depth, :])
+            f2[:depth, a * MAIN : (a + 1) * MAIN] = high
+            f2[depth:, a * MAIN : (a + 1) * MAIN] = low
+        for j in range(depth // 16):
             parts = [
-                sino_ref[group * GROUP + half * 8 + a][:, MAIN : MAIN + 2 * SIDE] for a in range(8)
+                sino_ref[group * GROUP + a, depth:, 16 * j : 16 * j + 16] for a in range(GROUP)
             ]
             high, low = split(jnp.concatenate(parts, axis=1))
-            own = slice(GROUP * MAIN + half * MAIN, GROUP * MAIN + (half + 1) * MAIN)
-            f2[:depth, own] = high
-            f2[depth:, own] = low
+            f2[16 * j : 16 * j + 16, GROUP * MAIN :] = high
+            f2[depth + 16 * j : depth + 16 * j + 16, GROUP * MAIN :] = low
         weights(group, jnp.int32(0), wh0, wl0)
 
         def two_pairs(step, inner):
@@ -233,7 +363,6 @@
     wide_count = lax.axis_size("wide")
     narrow_count = lax.axis_size("narrow")
     rows = projections.shape[1]
-    per_device = projections.shape[0]
     total = angle_index.shape[0]
     slab = rows // wide_count
     depth = -(-(slab + 12) // 16) * 16
@@ -246,13 +375,8 @@
             return min(max(first, 0), rows - depth)
         return jnp.minimum(jnp.maximum(first, 0), rows - depth)
 
-    windows = [filtered_window(projections[i], total) for i in range(per_device)]
-    window = jnp.stack(windows)
-    slabs = jnp.stack(
-        [window[:, z_start(w) : z_start(w) + depth] for w in range(wide_count) for n in range(narrow_count)]
-    )
-    sino = lax.all_to_all(slabs, ("wide", "narrow"), split_axis=0, concat_axis=0, tiled=True)
-    sino = sino.reshape(total, depth, 2 * MAIN)
+    starts = [z_start(w) for w in range(wide_count)]
+    sino = exchanged(projections, total, wide_count, depth, starts)
     angles = np.arange(total) * (math.pi / total)
     vmem = pl.BlockSpec(memory_space=pltpu.VMEM)
     smem = pl.BlockSpec(memory_space=pltpu.SMEM)
@@ -265,7 +389,7 @@
         scratch_shapes=[pltpu.VMEM((2 * depth, inner), bf16)]
         + [pltpu.VMEM((inner, 2 * XV), bf16)] * 4
         + [pltpu.VMEM((local_y, depth, XV), f32)],
-        compiler_params=pltpu.CompilerParams(vmem_limit_bytes=48 * 2**20),
+        compiler_params=pltpu.CompilerParams(vmem_limit_bytes=60 * 2**20),
         name="volume",
     )(
         angle_index,

time: 86.1 us -> 58.4 us (0.68)
  blocking collectives: 38.8 us -> 0 us
  Pallas kernels: 39.4 us -> 58.2 us
  local copies, waits for them, and re-layouts: 6.99 us -> 0 us
    all_to_all x1 -> x0, blocking collectives: 38.8 us -> none  [shards(): lax.all_to_all(slabs, ('wide', 'narrow'), split_axis=0, concat_axis=0, ti...]
    pallas_call x1, Pallas kernels: 7.31 us -> 25.5 us  [exchanged(): pl.pallas_call(functools.partial(exchange_kernel, (wide_count, depth, sta...]
    unnamed x35 -> x0, local copies, waits for them, and re-layouts: 6.98 us -> none
where the time goes in v2:
time: 58.4 us; the launch traced here: 58.2 us
  Pallas kernels  58.2 us (100%)
    pallas_call x1, Pallas kernels, shards(): pl.pallas_call(functools.partial(volume_kernel, (slab, tile_y, local_y, z...  32.7 us
    pallas_call x1, Pallas kernels, exchanged(): pl.pallas_call(functools.partial(exchange_kernel, (wide_count, depth, sta...  25.5 us

profile of v2, /device:TPU:0, one launch (start us, length us, event | category | flops | bytes accessed | tf_op | source)
XLA Modules:
  0.0 58.2 jit_solution(2361611252718034787)
XLA Ops:
  0.0 25.5 %filter_exchange.1.sino_ref = f32[16,96,128]{2,1,0:T(8,128)} custom-call(f32[1,512,512]{2,1,0:T(8,128)} %x_any.1, bf16[2,512,512]{2,1,0:T(8,128)(2,1)} %constant.12.clone.h_any, bf16[2,512,256]{2,1,0:T(8,128)(2,1)} %constant.13.clone.k_any, f32[512,128]{1,0:T(8,128)} %constant.14.clone.row_any, f32[1,512]{1,0:T(1,128)} %constant.15.clone.col_any), custom_call_target="tpu_custom_call" | custom-call | tf_op jit(solution)/shard_map/filter_exchange/pallas_call | solution.py:219
  25.5 32.7 %volume.1 = f32[64,32,128]{2,1,0:T(8,128)} custom-call(s32[16]{0:T(128)} %ang_ref.1, f32[16]{0:T(128)} %constant.16.clone.cos_ref, f32[16]{0:T(128)} %constant.17.clone.sin_ref, f32[16,96,128]{2,1,0:T(8,128)} %filter_exchange.1.sino_ref), custom_call_target="tpu_custom_call" | custom-call | tf_op jit(solution)/shard_map/volume/pallas_call | solution.py:384

commit v3 on v2

--- a/solution.py
+++ b/solution.py
@@ -58,6 +58,11 @@
 def split(value):
     high = value.astype(bf16)
     return high, (value - high.astype(f32)).astype(bf16)
+
+
+def stacked(value):
+    high = value.astype(bf16).astype(f32)
+    return jnp.concatenate([high, value - high], axis=0).astype(bf16)
 
 
 def dot3(left, right):
@@ -135,11 +140,13 @@
     for w, start in enumerate(starts):
         pack[w, :depth, :] = window[start : start + depth, :MAIN]
         sides = [
-            window[start + 16 * j : start + 16 * j + 16, MAIN : MAIN + 2 * SIDE]
-            for j in range(depth // 16)
+            window[start + j : start + min(j + 16, depth), MAIN : MAIN + 2 * SIDE]
+            for j in range(0, depth, 16)
         ]
-        pack[w, depth:, : depth] = jnp.concatenate(sides, axis=1)
-        pack[w, depth:, depth:] = jnp.zeros((16, MAIN - depth), f32)
+        if depth % 16:
+            sides[-1] = jnp.concatenate([sides[-1], jnp.zeros((8, 2 * SIDE), f32)], axis=0)
+        sides.append(jnp.zeros((16, MAIN - 16 * len(sides)), f32))
+        pack[w, depth:, :] = jnp.concatenate(sides, axis=1)
 
     pl.semaphore_wait(barrier, wide_count)
 
@@ -209,7 +216,7 @@
 def exchanged(projection, total, wide_count, depth, starts):
     rows, cols = projection.shape[1:]
     hartley = np.stack(halves(hartley_table(rows)))
-    ramp = np.stack(halves(ramp_table(cols, -math.pi / (attenuation * total))))
+    ramp = np.stack(halves(ramp_table(cols, -math.pi / (attenuation * total * contrast))))
     row_part = 1.0 + paganin_strength * 4.0 * np.sin(np.pi * np.arange(rows) / rows) ** 2
     col_part = paganin_strength * 4.0 * np.sin(np.pi * np.arange(cols) / cols) ** 2
     row_part = np.repeat(row_part[:, None].astype(np.float32), 128, axis=1)
@@ -250,14 +257,13 @@
 
 
 def conduct(diff):
-    base = 1.0 + diff * diff * (1.0 / contrast**2)
-    guess = pl.reciprocal(base, approx=True)
-    return diff * (guess * (2.0 - base * guess))
+    return diff * pl.reciprocal(1.0 + diff * diff, approx=True)
 
 
 def volume_kernel(plan, ang_ref, cos_ref, sin_ref, sino_ref, out_ref, f2, wh0, wl0, wh1, wl1, u):
     slab, tile_y, local_y, z_start, wide_count = plan
     total, depth = sino_ref.shape[0], sino_ref.shape[1] - 16
+    depth16 = -(-depth // 16) * 16
     wide_pos, narrow_pos = lax.axis_index("wide"), lax.axis_index("narrow")
     y_skip = tile_y - (local_y - tile_y)
     y_first = narrow_pos * y_skip
@@ -268,11 +274,11 @@
     cells = middle + [outer]
     centre = 0.5 * MAIN + SIDE - 0.5
 
-    def weights(group, pair, high_ref, low_ref):
+    def weights(group, pair, high_ref, low_ref, angles):
         for side in range(2):
             own = slice(side * XV, (side + 1) * XV)
             y_pos = (y_first + 2 * pair + side).astype(f32) + (0.5 - 0.5 * YV)
-            for a in range(GROUP):
+            for a in angles:
                 number = ang_ref[group * GROUP + a]
                 place = x_row * cos_ref[number] + (y_pos * sin_ref[number] + centre)
                 lower = jnp.floor(place)
@@ -293,10 +299,17 @@
                         is_here, left_fine, jnp.where(is_there, right_fine, zero)
                     )
 
-    def project(group, pair, high_ref, low_ref):
-        both = jnp.dot(f2[...], high_ref[...], preferred_element_type=f32)
-        rest = jnp.dot(f2[:depth, :], low_ref[...], preferred_element_type=f32)
-        value = both[:depth] + (both[depth:] + rest)
+    def project(group, pair, now_refs, later_refs):
+        both, rest = 0.0, 0.0
+        for part in range(GROUP * (MAIN + 2 * SIDE) // 256):
+            own = slice(256 * part, 256 * part + 256)
+            both = both + jnp.dot(f2[:, own], now_refs[0][own, :], preferred_element_type=f32)
+            rest = rest + jnp.dot(
+                f2[:depth16, own], now_refs[1][own, :], preferred_element_type=f32
+            )
+            if 2 * part < GROUP:
+                weights(group, pair + 1, *later_refs, (2 * part, 2 * part + 1))
+        value = both[:depth] + (both[depth:] + rest[:depth])
         for side in range(2):
             own = value[:, side * XV : (side + 1) * XV]
             if total > GROUP:
@@ -305,23 +318,21 @@
 
     def one_group(group, carry):
         for a in range(GROUP):
-            high, low = split(sino_ref[group * GROUP + a, :depth, :])
-            f2[:depth, a * MAIN : (a + 1) * MAIN] = high
-            f2[depth:, a * MAIN : (a + 1) * MAIN] = low
-        for j in range(depth // 16):
-            parts = [
-                sino_ref[group * GROUP + a, depth:, 16 * j : 16 * j + 16] for a in range(GROUP)
-            ]
-            high, low = split(jnp.concatenate(parts, axis=1))
-            f2[16 * j : 16 * j + 16, GROUP * MAIN :] = high
-            f2[depth + 16 * j : depth + 16 * j + 16, GROUP * MAIN :] = low
-        weights(group, jnp.int32(0), wh0, wl0)
+            own = sino_ref[group * GROUP + a, :depth, :]
+            f2[:, a * MAIN : (a + 1) * MAIN] = stacked(own)
+        sides = [
+            jnp.concatenate(
+                [sino_ref[group * GROUP + a, depth:, j : j + 16] for a in range(GROUP)], axis=1
+            )
+            for j in range(0, depth, 16)
+        ]
+        f2[:, GROUP * MAIN :] = stacked(jnp.concatenate(sides, axis=0)[:depth])
+        even, odd = (wh0, wl0), (wh1, wl1)
+        weights(group, jnp.int32(0), *even, range(GROUP))
 
         def two_pairs(step, inner):
-            weights(group, 2 * step + 1, wh1, wl1)
-            project(group, 2 * step, wh0, wl0)
-            weights(group, 2 * step + 2, wh0, wl0)
-            project(group, 2 * step + 1, wh1, wl1)
+            project(group, 2 * step, even, odd)
+            project(group, 2 * step + 1, odd, even)
             return inner
 
         lax.fori_loop(0, local_y // 4, two_pairs, 0)
@@ -349,14 +360,12 @@
         return later, flux_y
 
     for step in range(STEPS):
-        lax.fori_loop(0, local_y, row_step, (u[0], jnp.zeros((depth, XV), f32)), unroll=2)
+        lax.fori_loop(0, local_y, row_step, (u[0], jnp.zeros((depth, XV), f32)), unroll=12)
 
     z_skip = wide_pos * slab - z_start(wide_pos)
-    if slab % 8 == 0:
-        z_skip = pl.multiple_of(z_skip, 8)
     y_own = narrow_pos * (local_y - tile_y)
     for y in range(tile_y):
-        out_ref[:, y, :] = u[y_own + y, pl.ds(z_skip, slab), :]
+        out_ref[:, y, :] = u[y_own + y, pl.ds(z_skip, slab), :] * contrast
 
 
 def shards(projections, angle_index):
@@ -365,12 +374,12 @@
     rows = projections.shape[1]
     total = angle_index.shape[0]
     slab = rows // wide_count
-    depth = -(-(slab + 12) // 16) * 16
+    depth = -(-(slab + 2 * STEPS) // 8) * 8
     tile_y = YV // narrow_count
     local_y = tile_y + STEPS
 
     def z_start(wide_pos):
-        first = (wide_pos * slab + 8 - STEPS) // 8 * 8 - 8
+        first = wide_pos * slab - STEPS
         if isinstance(wide_pos, int):
             return min(max(first, 0), rows - depth)
         return jnp.minimum(jnp.maximum(first, 0), rows - depth)

time: 58.4 us -> 55.1 us (0.943)
  Pallas kernels: 58.2 us -> 54.9 us
    pallas_call x1, Pallas kernels: 32.7 us -> 30.1 us  [shards(): pl.pallas_call(functools.partial(volume_kernel, (slab, tile_y, local_y, z...]
    pallas_call x1, Pallas kernels: 25.5 us -> 24.8 us  [exchanged(): pl.pallas_call(functools.partial(exchange_kernel, (wide_count, depth, sta...]
where the time goes in v3:
time: 55.1 us; the launch traced here: 54.9 us
  Pallas kernels  54.9 us (100%)
    pallas_call x1, Pallas kernels, shards(): pl.pallas_call(functools.partial(volume_kernel, (slab, tile_y, local_y, z...  30.1 us
    pallas_call x1, Pallas kernels, exchanged(): pl.pallas_call(functools.partial(exchange_kernel, (wide_count, depth, sta...  24.8 us

profile of v3, /device:TPU:0, one launch (start us, length us, event | category | flops | bytes accessed | tf_op | source)
XLA Modules:
  0.0 54.9 jit_solution(8252474418228828065)
XLA Ops:
  0.0 24.8 %filter_exchange.1.sino_ref = f32[16,88,128]{2,1,0:T(8,128)} custom-call(f32[1,512,512]{2,1,0:T(8,128)} %x_any.1, bf16[2,512,512]{2,1,0:T(8,128)(2,1)} %constant.12.clone.h_any, bf16[2,512,256]{2,1,0:T(8,128)(2,1)} %constant.13.clone.k_any, f32[512,128]{1,0:T(8,128)} %constant.14.clone.row_any, f32[1,512]{1,0:T(1,128)} %constant.15.clone.col_any), custom_call_target="tpu_custom_call" | custom-call | tf_op jit(solution)/shard_map/filter_exchange/pallas_call | solution.py:226
  24.8 30.1 %volume.1 = f32[64,32,128]{2,1,0:T(8,128)} custom-call(s32[16]{0:T(128)} %ang_ref.1, f32[16]{0:T(128)} %constant.16.clone.cos_ref, f32[16]{0:T(128)} %constant.17.clone.sin_ref, f32[16,88,128]{2,1,0:T(8,128)} %filter_exchange.1.sino_ref), custom_call_target="tpu_custom_call" | custom-call | tf_op jit(solution)/shard_map/volume/pallas_call | solution.py:393
